TPU v7x, 128 devices: a whole 4x4x4 slice. The times are simulated.
128 devices in a mesh: series: 16 (over x, y), patch: 8 (over z, core).
Axes of the slice: x: 4, y: 4, z: 4, core: 2. Of those that a mesh axis runs over, the one named last changes fastest.
Arguments:
- series_data: bfloat16 [256, 512, 768], P(('series', 'patch')), may hold values from -6 to 6
- group_id: int32 [256], replicated, may hold values from 0 to 63, as said below
- gains: bfloat16 [3, 768], replicated, may hold values from 0.099609375 to 1.8984375
- w_time: bfloat16 [768, 2304], replicated, may hold values from -0.21875 to 0.21875
- w_time_out: bfloat16 [768, 768], replicated, may hold values from -0.21875 to 0.21875
- w_group: bfloat16 [768, 2304], replicated, may hold values from -0.21875 to 0.21875
- w_group_out: bfloat16 [768, 768], replicated, may hold values from -0.21875 to 0.21875
- w_up: bfloat16 [768, 3072], replicated, may hold values from -0.21875 to 0.21875
- w_down: bfloat16 [3072, 768], replicated, may hold values from -0.109375 to 0.109375
Outputs:
- layer_out: bfloat16 [256, 512, 768], P(('series', 'patch'))
Inputs may be any that keep to these rules, and one draw needn't show every extreme that they name: `group_id`: group ids never fall along the series and rise by at most one from a series to the next; a new group begins at every multiple of 16, and each aligned block of 16 series holds the same number of groups, a quarter of 16 but at least two; group sizes are ragged.
All inputs are finite; a program needn't handle non-finite values.
Results may differ from a plain program's by a relative error of at most 0.019.
Values may be sent and summed in bfloat16 or wider, within the bound.
No kernel may reach another device: no remote copies, remote signals or barrier semaphores. Data moves between devices by JAX's collectives and lax.ppermute only.
A program may use at most 128 MiB of HBM per device.

v0:
```python
import functools
import math

import jax
import jax.numpy as jnp
import numpy as np
from jax import lax
from jax.experimental import pallas as pl
from jax.experimental.pallas import tpu as pltpu
from jax.sharding import PartitionSpec as P

HEADS = 12
HEAD = 64
SLAB = 128
QUAD = 256
EPSILON = 1e-06
CHUNKS = 2
BLOCK = 16
BF16, F32 = jnp.bfloat16, jnp.float32
VMEM_LIMIT = 60 * 1024 * 1024

TAIL = (
    -1.0000376231361372,
    -1.1507878484871916,
    -0.4599924445285111,
    -0.05182737928832041,
    0.00708455624965549,
    -0.00047330922195818663,
)


def dot(a, b):
    return jnp.dot(a, b, preferred_element_type=F32)


def dot_t(a, b):
    return lax.dot_general(a, b, (((1,), (1,)), ((), ())), preferred_element_type=F32)


def normed(values, gain_row):
    values = values.astype(F32)
    mean_square = jnp.mean(values * values, axis=-1, keepdims=True)
    return (values * lax.rsqrt(mean_square + EPSILON) * gain_row).astype(BF16)


def gelu(x):
    size = jnp.abs(x)
    tail = jnp.full_like(size, TAIL[-1])
    for coefficient in TAIL[-2::-1]:
        tail = tail * size + coefficient
    return jnp.maximum(x, 0.0) - size * jnp.exp2(tail)


def rotary_tables(length):
    half = HEAD // 2
    frequency = 10000.0 ** (-np.arange(half) / half)
    angles = np.arange(length)[:, None] * frequency[None, :]
    cosine, sine = np.cos(angles), np.sin(angles)
    cosine = np.concatenate([cosine] * 4, axis=1).astype(np.float32)
    sine = np.concatenate([-sine, sine, -sine, sine], axis=1).astype(np.float32)
    return cosine, sine


def rotated(tensor, cosine, sine, scale=None):
    lane = lax.broadcasted_iota(jnp.int32, (tensor.shape[0], SLAB), 1)
    front = lax.rem(lane, HEAD) < HEAD // 2
    parts = []
    for start in range(0, tensor.shape[1], SLAB):
        slab = tensor[:, start : start + SLAB]
        other = jnp.where(front, pltpu.roll(slab, SLAB - 32, 1), pltpu.roll(slab, 32, 1))
        turned = slab * cosine + other * sine
        if scale is not None:
            turned = turned * scale
        parts.append(turned.astype(BF16))
    return jnp.concatenate(parts, axis=1)


QUERY_SCALE = math.log2(math.e) / math.sqrt(HEAD)
HBM = pl.BlockSpec(memory_space=pltpu.HBM)
SMEM = pl.BlockSpec(memory_space=pltpu.SMEM)


def slab_scores(queries, keys):
    first = lax.broadcasted_iota(jnp.int32, queries.shape, 1) < HEAD
    zero = jnp.zeros_like(queries)
    both = jnp.concatenate([jnp.where(first, queries, zero), jnp.where(first, zero, queries)], axis=0)
    return dot_t(both, keys)


def slab_context(scores, values):
    rows = scores.shape[0] // 2
    top = jnp.max(scores, axis=-1, keepdims=True)
    weights = jnp.exp2(scores - top).astype(BF16)
    sums = dot(weights, jnp.concatenate([values, jnp.ones_like(values)], axis=1))
    first = lax.broadcasted_iota(jnp.int32, (rows, SLAB), 1) < HEAD
    numerator = jnp.where(first, sums[:rows, :SLAB], sums[rows:, :SLAB])
    denominator = jnp.where(first, sums[:rows, SLAB:], sums[rows:, SLAB:])
    return (numerator / denominator).astype(BF16)


def pipelined(units, scores_of, context_of):
    scores = scores_of(units[0])
    for index, unit in enumerate(units):
        later = scores_of(units[index + 1]) if index + 1 < len(units) else None
        context_of(unit, scores)
        scores = later


def group_bias(ids, block):
    rows = block * BLOCK
    row = lax.broadcasted_iota(jnp.int32, (rows, rows), 0)
    column = lax.broadcasted_iota(jnp.int32, (rows, rows), 1)
    row_series, column_series = row // BLOCK, column // BLOCK
    row_group, column_group = jnp.zeros_like(row), jnp.zeros_like(row)
    first_series = lax.axis_index("series") * block
    for s in range(block):
        group = ids[first_series + s]
        row_group = jnp.where(row_series == s, group, row_group)
        column_group = jnp.where(column_series == s, group, column_group)
    same = jnp.logical_and(row_group == column_group, lax.rem(row, BLOCK) == lax.rem(column, BLOCK))
    return jnp.where(same, 0.0, -1e30)


class Copies:
    def __init__(self, sems):
        self.sems, self.used = sems, 0

    def start(self, source, target):
        copy = pltpu.make_async_copy(source, target, self.sems.at[self.used])
        self.used += 1
        copy.start()
        return copy


def time_kernel(chunk, *refs):
    if chunk == 0:
        (x_ref, gains_hbm, cos_hbm, sin_hbm, w_hbm, wo_hbm,
         mixed_ref, keys_hbm, values_hbm, later_hbm,
         x, wq, wo, cosine, sine, context, mixed, keys, values, norm, gains, wk, wv, sems) = refs
    else:
        (ids, x_ref, cos_hbm, sin_hbm, w_hbm, wo_hbm, keys_hbm, values_hbm, later_hbm,
         mixed_ref, bias_hbm, x, wq, wo, cosine, sine, context, mixed, keys, values, norm, bias, sems) = refs
    series, length, width = x_ref.shape
    part = length // CHUNKS
    low = chunk * part
    quads = width // QUAD
    copies = Copies(sems)
    puts = []
    needed = []
    if chunk == 0:
        get_gains = copies.start(gains_hbm, gains)
        get_x = [copies.start(x_ref.at[s], x.at[s]) for s in range(series)]
    else:
        get_norm = copies.start(later_hbm, norm)
    for j in range(quads):
        own = slice(j * QUAD, (j + 1) * QUAD)
        group = []
        for i, target in ((1, wk), (2, wv), (0, wq)) if chunk == 0 else ((0, wq),):
            lanes = slice(i * width + j * QUAD, i * width + (j + 1) * QUAD)
            group.append(copies.start(w_hbm.at[:, lanes], target.at[:, own]))
        if j == 0:
            group.append(copies.start(cos_hbm.at[low:], cosine))
            group.append(copies.start(sin_hbm.at[low:], sine))
        if chunk > 0:
            group.append(copies.start(keys_hbm.at[:, :, own], keys.at[:, :, own]))
            group.append(copies.start(values_hbm.at[:, :, own], values.at[:, :, own]))
        needed.append(group)
    get_wo = copies.start(wo_hbm, wo)
    if chunk == 0:
        get_gains.wait()
        gain = gains[0:1].astype(F32)
        for s in range(series):
            get_x[s].wait()
            norm[s] = normed(x[s], gain)
        puts.append(copies.start(norm.at[:, part:], later_hbm))
        now = norm[:, :part].reshape(series * part, width)
        everything = norm[...].reshape(series * length, width)
        residual = lambda s: x[s, :part]
    else:
        get_x = copies.start(x_ref.at[:, low:], x)
        bias[...] = group_bias(ids, mixed_ref.shape[0] * series)
        puts.append(copies.start(bias, bias_hbm))
        get_norm.wait()
        now = norm[...].reshape(series * part, width)
        residual = lambda s: x[s]
    for copy in needed[0] + needed[1] + needed[2] + [get_wo]:
        copy.wait()

    @pl.loop(0, quads)
    def _(j):
        own = pl.ds(pl.multiple_of(j * QUAD, QUAD), QUAD)
        if chunk == 0:
            raw = dot(everything, wk[:, own])
            own_values = dot(everything, wv[:, own]).astype(BF16).reshape(series, length, QUAD)
            own_keys = [
                rotated(raw[s * length : (s + 1) * length], cosine[...], sine[...]) for s in range(series)
            ]
            values[:, :, own] = own_values
            for s in range(series):
                keys[s, :, own] = own_keys[s]
        else:
            own_values = values[:, :, own]
            own_keys = [keys[s, :, own] for s in range(series)]
        raw = dot(now, wq[:, own])
        queries = [
            rotated(raw[s * part : (s + 1) * part], cosine[:part], sine[:part], QUERY_SCALE)
            for s in range(series)
        ]

        def scores_of(unit):
            start, s = unit
            lanes = slice(start, start + SLAB)
            return slab_scores(queries[s][:, lanes], own_keys[s][:, lanes])

        def context_of(unit, scores):
            start, s = unit
            made = slab_context(scores, own_values[s][:, start : start + SLAB])
            target = pl.ds(pl.multiple_of(j * QUAD + start, SLAB), SLAB)
            context[s * part : (s + 1) * part, target] = made

        pipelined([(start, s) for start in range(0, QUAD, SLAB) for s in range(series)], scores_of, context_of)

    if chunk == 0:
        puts.append(copies.start(keys, keys_hbm))
        puts.append(copies.start(values, values_hbm))
    if chunk > 0:
        get_x.wait()
    update = dot(context[...], wo[...])
    for s in range(series):
        result = residual(s).astype(F32) + update[s * part : (s + 1) * part]
        mixed[s] = result.astype(BF16).reshape(mixed.shape[1:])
        puts.append(copies.start(mixed.at[s], mixed_ref.at[:, s]))
    for put in puts:
        put.wait()


def params(mebibytes=60):
    return pltpu.CompilerParams(vmem_limit_bytes=mebibytes * 1024 * 1024)


def time_chunk(chunk, devices, x, gains, tables, w_time, w_time_out, ids=None, kept=()):
    series, length, width = x.shape
    part = length // CHUNKS
    mixed_shape = (devices, series, part // devices, width)
    rows = series * part
    table_rows = length - chunk * part
    like = jax.ShapeDtypeStruct(x.shape, BF16)
    out_shape = [jax.ShapeDtypeStruct(mixed_shape, BF16)]
    operands = [x, *tables, w_time, w_time_out, *kept]
    scratch = [
        pltpu.VMEM((series, length if chunk == 0 else part, width), BF16),
        pltpu.VMEM((width, width), BF16),
        pltpu.VMEM((width, width), BF16),
        pltpu.VMEM((table_rows, SLAB), F32),
        pltpu.VMEM((table_rows, SLAB), F32),
        pltpu.VMEM((rows, width), BF16),
        pltpu.VMEM((series, devices, part // devices, width), BF16),
        pltpu.VMEM(x.shape, BF16),
        pltpu.VMEM(x.shape, BF16),
        pltpu.VMEM((series, length if chunk == 0 else part, width), BF16),
    ]
    flops = 2 * rows * width * width * 2 + 8 * rows * length * width
    if chunk == 0:
        in_specs = [HBM] * 6
        operands.insert(1, gains)
        out_shape += [like, like, jax.ShapeDtypeStruct((series, length - part, width), BF16)]
        scratch += [
            pltpu.VMEM(gains.shape, BF16),
            pltpu.VMEM((width, width), BF16),
            pltpu.VMEM((width, width), BF16),
        ]
        flops += 2 * series * length * width * width * 2
    else:
        pairs = (devices * series * BLOCK,) * 2
        in_specs = [SMEM] + [HBM] * len(operands)
        operands.insert(0, ids)
        out_shape.append(jax.ShapeDtypeStruct(pairs, F32))
        scratch.append(pltpu.VMEM(pairs, F32))
    return pl.pallas_call(
        functools.partial(time_kernel, chunk),
        in_specs=in_specs,
        out_specs=[HBM] * len(out_shape),
        out_shape=out_shape,
        scratch_shapes=scratch + [pltpu.SemaphoreType.DMA((32,))],
        compiler_params=params(),
        cost_estimate=pl.CostEstimate(
            flops=flops, bytes_accessed=8 << 20, transcendentals=rows * length * HEADS
        ),
        name=f"time_attention_{chunk}",
    )(*operands)


FF_TILE = 256


FF_BODY = 1024


def feed(norm, up, down, total):
    @pl.loop(0, up.shape[1] // FF_BODY)
    def _(j):
        hidden = []
        for start in range(0, FF_BODY, FF_TILE):
            own = pl.ds(pl.multiple_of(j * FF_BODY + start, FF_TILE), FF_TILE)
            hidden.append(gelu(dot(norm[...], up[:, own])).astype(BF16))
        own = pl.ds(pl.multiple_of(j * FF_BODY, FF_BODY), FF_BODY)
        total[...] += dot(jnp.concatenate(hidden, axis=1), down[own, :])


def group_kernel(chunk, *refs):
    if chunk == 0:
        (bias_hbm, x_ref, gains_hbm, wg_hbm, wo_hbm, out_ref,
         x, norm, context, result, bias, gains, wg, wo, sems) = refs
    else:
        (bias_hbm, x_ref, gains_hbm, wg_hbm, wo_hbm, up_hbm, down_hbm, out_ref,
         x, norm, context, result, bias, gains, wg, wo, hidden, up, down, sems) = refs
    block, patches, width = x_ref.shape
    tiles = patches // BLOCK
    rows = block * BLOCK
    copies = Copies(sems)
    patches_of = lambda t: slice(t * BLOCK, (t + 1) * BLOCK)
    rows_of = lambda t: slice(t * rows, (t + 1) * rows)
    get_x = [copies.start(gains_hbm, gains)]
    get_x += [copies.start(x_ref.at[:, patches_of(t)], x.at[t]) for t in range(tiles)]
    quads = width // QUAD
    get_w = []
    for j in range(quads):
        parts = [slice(i * width + j * QUAD, i * width + (j + 1) * QUAD) for i in range(3)]
        get_w.append([copies.start(wg_hbm.at[:, lanes], wg.at[:, lanes]) for lanes in parts])
        if j == 0:
            get_w[0].append(copies.start(bias_hbm, bias))
    get_w[-1].append(copies.start(wo_hbm, wo))
    if chunk > 0:
        get_feed = [copies.start(up_hbm, up), copies.start(down_hbm, down)]

    get_x[0].wait()
    gain = gains[1:2].astype(F32)
    for t in range(tiles):
        get_x[1 + t].wait()
        norm[rows_of(t)] = normed(x[t].reshape(rows, width), gain)
    for copies_of_quad in get_w:
        for copy in copies_of_quad:
            copy.wait()

    @pl.loop(0, quads)
    def _(j):
        def project(i):
            return dot(norm[...], wg[:, pl.ds(pl.multiple_of(i * width + j * QUAD, QUAD), QUAD)])

        queries = (project(0) * QUERY_SCALE).astype(BF16)
        own_keys = project(1).astype(BF16)
        own_values = project(2).astype(BF16)

        def scores_of(unit):
            start, t = unit
            lanes = slice(start, start + SLAB)
            scores = slab_scores(queries[rows_of(t), lanes], own_keys[rows_of(t), lanes])
            return scores + jnp.concatenate([bias[...], bias[...]], axis=0)

        def context_of(unit, scores):
            start, t = unit
            made = slab_context(scores, own_values[rows_of(t), start : start + SLAB])
            context[rows_of(t), pl.ds(pl.multiple_of(j * QUAD + start, SLAB), SLAB)] = made

        pipelined([(start, t) for start in range(0, QUAD, SLAB) for t in range(tiles)], scores_of, context_of)

    if chunk > 0:
        for copy in get_feed:
            copy.wait()
    update = dot(context[...], wo[...])
    if chunk > 0:
        gain = gains[2:3].astype(F32)
        for t in range(tiles):
            total = x[t].reshape(rows, width).astype(F32) + update[rows_of(t)]
            x[t] = total.astype(BF16).reshape(block, BLOCK, width)
            norm[rows_of(t)] = normed(x[t].reshape(rows, width), gain)
            hidden[rows_of(t)] = x[t].reshape(rows, width).astype(F32)
        feed(norm, up, down, hidden)
    puts = []
    for t in range(tiles):
        if chunk > 0:
            total = hidden[rows_of(t)]
        else:
            total = x[t].reshape(rows, width).astype(F32) + update[rows_of(t)]
        result[t] = total.astype(BF16).reshape(block, BLOCK, width)
        puts.append(copies.start(result.at[t], out_ref.at[:, patches_of(t)]))
    for copy in puts:
        copy.wait()


def group_chunk(chunk, x, bias, gains, w_group, w_group_out, *feed_weights):
    block, patches, width = x.shape
    rows = block * patches
    tiles = (patches // BLOCK, block, BLOCK, width)
    extra = [pltpu.VMEM(array.shape, BF16) for array in feed_weights]
    if extra:
        extra.insert(0, pltpu.VMEM((rows, width), F32))
    return pl.pallas_call(
        functools.partial(group_kernel, chunk),
        in_specs=[HBM] * (5 + len(feed_weights)),
        out_specs=HBM,
        out_shape=jax.ShapeDtypeStruct(x.shape, BF16),
        scratch_shapes=[
            pltpu.VMEM(tiles, BF16),
            pltpu.VMEM((rows, width), BF16),
            pltpu.VMEM((rows, width), BF16),
            pltpu.VMEM(tiles, BF16),
            pltpu.VMEM(bias.shape, F32),
            pltpu.VMEM(gains.shape, BF16),
            pltpu.VMEM(w_group.shape, BF16),
            pltpu.VMEM(w_group_out.shape, BF16),
            *extra,
            pltpu.SemaphoreType.DMA((20,)),
        ],
        compiler_params=params(),
        cost_estimate=pl.CostEstimate(
            flops=2 * rows * width * width * (4 + 8 * chunk) + 8 * rows * 256 * width,
            bytes_accessed=8 << 20,
            transcendentals=rows * 256 * HEADS,
        ),
        name=f"group_attention_{chunk}",
    )(bias, x, gains, w_group, w_group_out, *feed_weights)


def feed_kernel(x_ref, gains_hbm, up_hbm, down_hbm, out_ref, x, norm, hidden, result, gains, up, down, sems):
    devices, series, patches, width = x_ref.shape
    rows = devices * patches
    rows_of = lambda s: slice(s * rows, (s + 1) * rows)
    copies = Copies(sems)
    get_gains = copies.start(gains_hbm, gains)
    get_x = [copies.start(x_ref.at[:, s], x.at[s]) for s in range(series)]
    get_feed = [copies.start(up_hbm, up), copies.start(down_hbm, down)]
    get_gains.wait()
    gain = gains[2:3].astype(F32)
    for s in range(series):
        get_x[s].wait()
        norm[rows_of(s)] = normed(x[s].reshape(rows, width), gain)
        hidden[rows_of(s)] = x[s].reshape(rows, width).astype(F32)
    for copy in get_feed:
        copy.wait()
    feed(norm, up, down, hidden)
    puts = []
    for s in range(series):
        result[s] = hidden[rows_of(s)].astype(BF16)
        puts.append(copies.start(result.at[s], out_ref.at[s, :rows]))
    for put in puts:
        put.wait()


def feed_chunk(x, gains, w_up, w_down):
    devices, series, patches, width = x.shape
    hidden = w_up.shape[1]
    part = devices * patches
    rows = series * part
    return pl.pallas_call(
        feed_kernel,
        in_specs=[HBM] * 4,
        out_specs=HBM,
        out_shape=jax.ShapeDtypeStruct((series, CHUNKS * part, width), BF16),
        scratch_shapes=[
            pltpu.VMEM((series, devices, patches, width), BF16),
            pltpu.VMEM((rows, width), BF16),
            pltpu.VMEM((rows, width), F32),
            pltpu.VMEM((series, part, width), BF16),
            pltpu.VMEM(gains.shape, BF16),
            pltpu.VMEM(w_up.shape, BF16),
            pltpu.VMEM(w_down.shape, BF16),
            pltpu.SemaphoreType.DMA((20,)),
        ],
        compiler_params=params(),
        cost_estimate=pl.CostEstimate(
            flops=4 * rows * width * hidden, bytes_accessed=4 << 20, transcendentals=rows * hidden
        ),
        name="feed_forward_0",
    )(x, gains, w_up, w_down)


def place_kernel(x_ref, _, out_ref, x, get_sems, put_sems):
    series = x_ref.shape[1]
    low = out_ref.shape[1] // CHUNKS
    gets, puts = Copies(get_sems), Copies(put_sems)
    arrivals = [gets.start(x_ref.at[:, s], x.at[s]) for s in range(series)]
    leaving = []
    for s in range(series):
        arrivals[s].wait()
        rows = x.at[s].reshape(low, out_ref.shape[2])
        leaving.append(puts.start(rows, out_ref.at[s, low:]))
    for copy in leaving:
        copy.wait()


def placed(x, out):
    devices, series, patches, width = x.shape
    return pl.pallas_call(
        place_kernel,
        in_specs=[HBM] * 2,
        out_specs=HBM,
        out_shape=jax.ShapeDtypeStruct(out.shape, BF16),
        scratch_shapes=[
            pltpu.VMEM((series, devices, patches, width), BF16),
            pltpu.SemaphoreType.DMA((series,)),
            pltpu.SemaphoreType.DMA((series,)),
        ],
        input_output_aliases={1: 0},
        compiler_params=pltpu.CompilerParams(vmem_limit_bytes=4 << 20),
        name="rows_in_place",
    )(x, out)


def exchanged(blocks):
    return lax.all_to_all(blocks, "patch", split_axis=0, concat_axis=0)


def per_device(
    series_data, group_id, gains, w_time, w_time_out, w_group, w_group_out, w_up, w_down
):
    devices = lax.axis_size("patch")
    series, length, width = series_data.shape
    block = devices * series
    tables = rotary_tables(length)

    time_inputs = (devices, series_data, gains, tables, w_time, w_time_out)
    mixed_a, *kept = time_chunk(0, *time_inputs)
    there_a = exchanged(mixed_a)
    mixed_b, bias = time_chunk(1, *time_inputs, group_id, kept)
    there_b = exchanged(mixed_b)
    shape = there_a.shape
    joined = (block, shape[2], width)
    group_inputs = (bias, gains, w_group, w_group_out)
    group_a = group_chunk(0, there_a.reshape(joined), *group_inputs)
    back_a = exchanged(group_a.reshape(shape))
    group_b = group_chunk(1, there_b.reshape(joined), *group_inputs, w_up, w_down)
    back_b = exchanged(group_b.reshape(shape))
    out = feed_chunk(back_a, gains, w_up, w_down)
    return placed(back_b, out)


def solution(mesh):
    in_specs = (P(("series", "patch"), None, None), P(), P(), P(), P(), P(), P(), P(), P())
    out_specs = P(("series", "patch"), None, None)
    return jax.shard_map(
        per_device, mesh=mesh, in_specs=in_specs, out_specs=out_specs, check_vma=False
    )
```

profile of v0, /device:TPU:1, one launch (start us, length us, event | category | flops | bytes accessed | tf_op | source)
XLA Modules:
  0.0 88.6 jit_solution(3121075759488805785)
XLA Ops:
  0.0 13.9 %time_attention_0.1 = (bf16[8,2,32,768]{3,2,1,0:T(8,128)(2,1)}, bf16[2,512,768]{2,1,0:T(8,128)(2,1)}, bf16[2,512,768]{2,1,0:T(8,128)(2,1)}, bf16[2,256,768]{2,1,0:T(8,128)(2,1)}) custom-call(bf16[2,512,768]{2,1,0:T(8,128)(2,1)} %refs_1_.3, bf16[3,768]{1,0:T(4,128)(2,1)} %gains_hbm.1, f32[512,128]{1,0:T(8,128)} %constant.4.clone.refs_2_, ...), custom_call_target="tpu_custom_call" | custom-call | flops 5234491392 | bytes 8388608 | tf_op jit(solution)/shard_map/time_attention_0/pallas_call | solution.py:279
  14.0 6.8 %all-to-all-start.2 = ((bf16[8,2,32,768]{3,2,1,0:T(8,128)(2,1)}), bf16[8,2,32,768]{3,2,1,0:T(8,128)(2,1)S(1)}, u32[]{:S(2)}, u32[]{:S(2)}) async-start(bf16[8,2,32,768]{3,2,1,0:T(8,128)(2,1)} %get-tuple-element.16), calls=%async_computation.2 | async-start | bytes 1572864 | tf_op jit(solution)/shard_map/all_to_all | solution.py:511
  20.8 11.6 %time_attention_1.1 = (bf16[8,2,32,768]{3,2,1,0:T(8,128)(2,1)}, f32[256,256]{1,0:T(8,128)}) custom-call(s32[256]{0:T(256)} %refs_0_.3, bf16[2,512,768]{2,1,0:T(8,128)(2,1)} %refs_1_.3, f32[512,128]{1,0:T(8,128)} %constant.4.clone.refs_2_, f32[512,128]{1,0:T(8,128)} %constant.5.clone.refs_3_, bf16[768,2304]{1,0:T(8,128)(2,1)} %refs_4_.5, ...), custom_call_target="tpu_custom_call" | custom-call | flops 2818572288 | bytes 8388608 | tf_op jit(solution)/shard_map/time_attention_1/pallas_call | solution.py:279
  32.4 0.7 all-to-all-done.2
  33.1 0.0 copy-start
  33.1 4.3 %all-to-all-start = ((bf16[8,2,32,768]{3,2,1,0:T(8,128)(2,1)}), bf16[8,2,32,768]{3,2,1,0:T(8,128)(2,1)S(1)}, u32[]{:S(2)}, u32[]{:S(2)}) async-start(bf16[8,2,32,768]{3,2,1,0:T(8,128)(2,1)} %get-tuple-element.15), calls=%async_computation | async-start | bytes 1572864 | tf_op jit(solution)/shard_map/all_to_all | solution.py:511
  37.4 0.0 copy-done
  37.4 8.9 %group_attention_0.1 = bf16[16,32,768]{2,1,0:T(8,128)(2,1)} custom-call(f32[256,256]{1,0:T(8,128)} %get-tuple-element.14.refs_0_, bf16[16,32,768]{2,1,0:T(8,128)(2,1)} %bitcast.4, bf16[3,768]{1,0:T(4,128)(2,1)} %gains_hbm.1, bf16[768,2304]{1,0:T(8,128)(2,1)} %refs_3_.5, bf16[768,768]{1,0:T(8,128)(2,1)} %refs_4_.7), custom_call_target="tpu_custom_call" | custom-call | flops 3221225472 | bytes 8388608 | tf_op jit(solution)/shard_map/group_attention_0/pallas_call | solution.py:398
  46.3 3.4 %all-to-all-done = bf16[8,2,32,768]{3,2,1,0:T(8,128)(2,1)S(1)} async-done(((bf16[8,2,32,768]{3,2,1,0:T(8,128)(2,1)}), bf16[8,2,32,768]{3,2,1,0:T(8,128)(2,1)S(1)}, u32[]{:S(2)}, u32[]{:S(2)}) %all-to-all-start) | async-done | bytes 786464 | tf_op jit(solution)/shard_map/all_to_all | solution.py:511
  49.7 0.0 copy-start.1
  49.7 4.3 %all-to-all-start.3 = ((bf16[8,2,32,768]{3,2,1,0:T(8,128)(2,1)}), bf16[8,2,32,768]{3,2,1,0:T(8,128)(2,1)S(1)}, u32[]{:S(2)}, u32[]{:S(2)}) async-start(bf16[8,2,32,768]{3,2,1,0:T(8,128)(2,1)} %bitcast.6), calls=%async_computation.3 | async-start | bytes 1572864 | tf_op jit(solution)/shard_map/all_to_all | solution.py:511
  54.0 0.0 copy-done.1
  54.0 16.3 %group_attention_1.1 = bf16[16,32,768]{2,1,0:T(8,128)(2,1)} custom-call(f32[256,256]{1,0:T(8,128)} %get-tuple-element.14.refs_0_, bf16[16,32,768]{2,1,0:T(8,128)(2,1)} %bitcast.5, bf16[3,768]{1,0:T(4,128)(2,1)} %gains_hbm.1, bf16[768,2304]{1,0:T(8,128)(2,1)} %refs_3_.5, bf16[768,768]{1,0:T(8,128)(2,1)} %refs_4_.7, bf16[768,3072]{1,0:T(8,128)(2,1)} %up_hbm.1, ...), custom_call_target="tpu_custom_call" | custom-call | flops 8053063680 | bytes 8388608 | tf_op jit(solution)/shard_map/group_attention_1/pallas_call | solution.py:398
  70.3 0.0 all-to-all-done.3.x_ref
  70.3 0.0 copy-start.2
  70.3 4.8 %all-to-all-start.1 = ((bf16[8,2,32,768]{3,2,1,0:T(8,128)(2,1)}), bf16[8,2,32,768]{3,2,1,0:T(8,128)(2,1)S(1)}, u32[]{:S(2)}, u32[]{:S(2)}) async-start(bf16[8,2,32,768]{3,2,1,0:T(8,128)(2,1)} %bitcast.7), calls=%async_computation.1 | async-start | bytes 1572864 | tf_op jit(solution)/shard_map/all_to_all | solution.py:511
  75.2 0.0 copy-done.2
  75.2 12.2 %feed_forward_0.1._ = bf16[2,512,768]{2,1,0:T(8,128)(2,1)} custom-call(bf16[8,2,32,768]{3,2,1,0:T(8,128)(2,1)} %copy-done.2, bf16[3,768]{1,0:T(4,128)(2,1)} %gains_hbm.1, bf16[768,3072]{1,0:T(8,128)(2,1)} %up_hbm.1, bf16[3072,768]{1,0:T(8,128)(2,1)} %down_hbm.1), custom_call_target="tpu_custom_call" | custom-call | flops 4831838208 | bytes 4194304 | tf_op jit(solution)/shard_map/feed_forward_0/pallas_call | solution.py:455
  87.3 0.1 all-to-all-done.1.x_ref
  87.5 1.0 %rows_in_place.1 = bf16[2,512,768]{2,1,0:T(8,128)(2,1)} custom-call(bf16[8,2,32,768]{3,2,1,0:T(8,128)(2,1)S(1)} %all-to-all-done.1.x_ref, bf16[2,512,768]{2,1,0:T(8,128)(2,1)} %feed_forward_0.1._), custom_call_target="tpu_custom_call", output_to_operand_aliasing={{}: (1, {})} | custom-call | tf_op jit(solution)/shard_map/rows_in_place/pallas_call | solution.py:494
Async XLA Ops:
  14.0 19.1 %all-to-all-start.2 = ((bf16[8,2,32,768]{3,2,1,0:T(8,128)(2,1)}), bf16[8,2,32,768]{3,2,1,0:T(8,128)(2,1)S(1)}, u32[]{:S(2)}, u32[]{:S(2)}) async-start(bf16[8,2,32,768]{3,2,1,0:T(8,128)(2,1)} %get-tuple-element.16), calls=%async_computation.2 | async-start | bytes 1572864 | tf_op jit(solution)/shard_map/all_to_all | solution.py:511
  33.1 4.3 %copy-start = (bf16[8,2,32,768]{3,2,1,0:T(8,128)(2,1)}, bf16[8,2,32,768]{3,2,1,0:T(8,128)(2,1)S(1)}, u32[]{:S(2)}) copy-start(bf16[8,2,32,768]{3,2,1,0:T(8,128)(2,1)S(1)} %all-to-all-done.2) | copy-start | bytes 2359300
  33.1 16.6 %all-to-all-start = ((bf16[8,2,32,768]{3,2,1,0:T(8,128)(2,1)}), bf16[8,2,32,768]{3,2,1,0:T(8,128)(2,1)S(1)}, u32[]{:S(2)}, u32[]{:S(2)}) async-start(bf16[8,2,32,768]{3,2,1,0:T(8,128)(2,1)} %get-tuple-element.15), calls=%async_computation | async-start | bytes 1572864 | tf_op jit(solution)/shard_map/all_to_all | solution.py:511
  49.7 4.3 %copy-start.1 = (bf16[8,2,32,768]{3,2,1,0:T(8,128)(2,1)}, bf16[8,2,32,768]{3,2,1,0:T(8,128)(2,1)S(1)}, u32[]{:S(2)}) copy-start(bf16[8,2,32,768]{3,2,1,0:T(8,128)(2,1)S(1)} %all-to-all-done) | copy-start | bytes 2359300
  49.7 20.6 %all-to-all-start.3 = ((bf16[8,2,32,768]{3,2,1,0:T(8,128)(2,1)}), bf16[8,2,32,768]{3,2,1,0:T(8,128)(2,1)S(1)}, u32[]{:S(2)}, u32[]{:S(2)}) async-start(bf16[8,2,32,768]{3,2,1,0:T(8,128)(2,1)} %bitcast.6), calls=%async_computation.3 | async-start | bytes 1572864 | tf_op jit(solution)/shard_map/all_to_all | solution.py:511
  70.3 4.8 %copy-start.2 = (bf16[8,2,32,768]{3,2,1,0:T(8,128)(2,1)}, bf16[8,2,32,768]{3,2,1,0:T(8,128)(2,1)S(1)}, u32[]{:S(2)}) copy-start(bf16[8,2,32,768]{3,2,1,0:T(8,128)(2,1)S(1)} %all-to-all-done.3.x_ref) | copy-start | bytes 2359300
  70.3 17.1 %all-to-all-start.1 = ((bf16[8,2,32,768]{3,2,1,0:T(8,128)(2,1)}), bf16[8,2,32,768]{3,2,1,0:T(8,128)(2,1)S(1)}, u32[]{:S(2)}, u32[]{:S(2)}) async-start(bf16[8,2,32,768]{3,2,1,0:T(8,128)(2,1)} %bitcast.7), calls=%async_computation.1 | async-start | bytes 1572864 | tf_op jit(solution)/shard_map/all_to_all | solution.py:511
where the time goes:
time: 89 us; the launch traced here: 88.6 us
  Pallas kernels  63.8 us (72%)
  starting transfers between devices  20.3 us (23%)
  waiting for transfers between devices  4.23 us (5%)
    pallas_call x2, Pallas kernels, time_chunk(): pl.pallas_call(functools.partial(time_kernel, chunk), in_specs=in_specs,...  25.5 us
    pallas_call x2, Pallas kernels, group_chunk(): pl.pallas_call(functools.partial(group_kernel, chunk), in_specs=[HBM] * (...  25.2 us
    all_to_all x4, starting transfers between devices, exchanged(): return lax.all_to_all(blocks, 'patch', split_axis=0, concat_axis=0)  20.3 us
    pallas_call x1, Pallas kernels, feed_chunk(): pl.pallas_call(feed_kernel, in_specs=[HBM] * 4, out_specs=HBM, out_shape=...  12.2 us
    all_to_all x4, waiting for transfers between devices, exchanged(): return lax.all_to_all(blocks, 'patch', split_axis=0, concat_axis=0)  4.23 us
  transfers between devices with their start and end apart: 4, of which 3 were waited for; matrix products, arithmetic and copies ran while one was open for 0% of the time, Pallas kernels for 55%

commit v1 on v0

--- a/solution.py
+++ b/solution.py
@@ -183,46 +183,71 @@
         get_norm.wait()
         now = norm[...].reshape(series * part, width)
         residual = lambda s: x[s]
-    for copy in needed[0] + needed[1] + needed[2] + [get_wo]:
-        copy.wait()
-
-    @pl.loop(0, quads)
-    def _(j):
-        own = pl.ds(pl.multiple_of(j * QUAD, QUAD), QUAD)
-        if chunk == 0:
+    if chunk == 0:
+        lanes_of = lambda j: slice(j * QUAD, (j + 1) * QUAD)
+        queries = {}
+
+        def project(j):
+            own = lanes_of(j)
             raw = dot(everything, wk[:, own])
-            own_values = dot(everything, wv[:, own]).astype(BF16).reshape(series, length, QUAD)
-            own_keys = [
-                rotated(raw[s * length : (s + 1) * length], cosine[...], sine[...]) for s in range(series)
-            ]
-            values[:, :, own] = own_values
             for s in range(series):
-                keys[s, :, own] = own_keys[s]
-        else:
+                keys[s, :, own] = rotated(raw[s * length : (s + 1) * length], cosine[...], sine[...])
+            values[:, :, own] = dot(everything, wv[:, own]).astype(BF16).reshape(series, length, QUAD)
+            raw = dot(now, wq[:, own])
+            for s in range(series):
+                rows = raw[s * part : (s + 1) * part]
+                queries[j, s] = rotated(rows, cosine[:part], sine[:part], QUERY_SCALE)
+
+        def scores_of(unit):
+            j, start, s = unit
+            own = slice(j * QUAD + start, j * QUAD + start + SLAB)
+            return slab_scores(queries[j, s][:, start : start + SLAB], keys[s, :, own])
+
+        def context_of(unit, scores):
+            j, start, s = unit
+            own = slice(j * QUAD + start, j * QUAD + start + SLAB)
+            context[s * part : (s + 1) * part, own] = slab_context(scores, values[s, :, own])
+
+        for copy in needed[0]:
+            copy.wait()
+        project(0)
+        for copy in needed[1] + needed[2] + [get_wo]:
+            copy.wait()
+        for j in range(quads):
+            if j + 1 < quads:
+                project(j + 1)
+            pipelined([(j, start, s) for start in range(0, QUAD, SLAB) for s in range(series)], scores_of, context_of)
+            if j + 2 == quads:
+                puts.append(copies.start(keys, keys_hbm))
+                puts.append(copies.start(values, values_hbm))
+    else:
+        for copy in needed[0] + needed[1] + needed[2] + [get_wo]:
+            copy.wait()
+
+        @pl.loop(0, quads)
+        def _(j):
+            own = pl.ds(pl.multiple_of(j * QUAD, QUAD), QUAD)
             own_values = values[:, :, own]
             own_keys = [keys[s, :, own] for s in range(series)]
-        raw = dot(now, wq[:, own])
-        queries = [
-            rotated(raw[s * part : (s + 1) * part], cosine[:part], sine[:part], QUERY_SCALE)
-            for s in range(series)
-        ]
-
-        def scores_of(unit):
-            start, s = unit
-            lanes = slice(start, start + SLAB)
-            return slab_scores(queries[s][:, lanes], own_keys[s][:, lanes])
-
-        def context_of(unit, scores):
-            start, s = unit
-            made = slab_context(scores, own_values[s][:, start : start + SLAB])
-            target = pl.ds(pl.multiple_of(j * QUAD + start, SLAB), SLAB)
-            context[s * part : (s + 1) * part, target] = made
-
-        pipelined([(start, s) for start in range(0, QUAD, SLAB) for s in range(series)], scores_of, context_of)
-
-    if chunk == 0:
-        puts.append(copies.start(keys, keys_hbm))
-        puts.append(copies.start(values, values_hbm))
+            raw = dot(now, wq[:, own])
+            queries = [
+                rotated(raw[s * part : (s + 1) * part], cosine[:part], sine[:part], QUERY_SCALE)
+                for s in range(series)
+            ]
+
+            def scores_of(unit):
+                start, s = unit
+                lanes = slice(start, start + SLAB)
+                return slab_scores(queries[s][:, lanes], own_keys[s][:, lanes])
+
+            def context_of(unit, scores):
+                start, s = unit
+                made = slab_context(scores, own_values[s][:, start : start + SLAB])
+                target = pl.ds(pl.multiple_of(j * QUAD + start, SLAB), SLAB)
+                context[s * part : (s + 1) * part, target] = made
+
+            pipelined([(start, s) for start in range(0, QUAD, SLAB) for s in range(series)], scores_of, context_of)
+
     if chunk > 0:
         get_x.wait()
     update = dot(context[...], wo[...])

time: 89 us -> 87.1 us (0.979)
  Pallas kernels: 63.8 us -> 61.9 us
    pallas_call x2, Pallas kernels: 25.5 us -> 23.6 us  [time_chunk(): pl.pallas_call(functools.partial(time_kernel, chunk), in_specs=in_specs,...]
  transfers between devices with their start and end apart: 4 -> 4, of which waited for: 3 -> 3; matrix products, arithmetic and copies ran while one was open for 0% -> 0% of each run, Pallas kernels for 55% -> 56%
where the time goes in v1:
time: 87.1 us; the launch traced here: 86.7 us
  Pallas kernels  61.9 us (71%)
  starting transfers between devices  20.3 us (23%)
  waiting for transfers between devices  4.22 us (5%)
    pallas_call x2, Pallas kernels, group_chunk(): pl.pallas_call(functools.partial(group_kernel, chunk), in_specs=[HBM] * (...  25.2 us
    pallas_call x2, Pallas kernels, time_chunk(): pl.pallas_call(functools.partial(time_kernel, chunk), in_specs=in_specs,...  23.6 us
    all_to_all x4, starting transfers between devices, exchanged(): return lax.all_to_all(blocks, 'patch', split_axis=0, concat_axis=0)  20.3 us
    pallas_call x1, Pallas kernels, feed_chunk(): pl.pallas_call(feed_kernel, in_specs=[HBM] * 4, out_specs=HBM, out_shape=...  12.2 us
    all_to_all x4, waiting for transfers between devices, exchanged(): return lax.all_to_all(blocks, 'patch', split_axis=0, concat_axis=0)  4.22 us
  transfers between devices with their start and end apart: 4, of which 3 were waited for; matrix products, arithmetic and copies ran while one was open for 0% of the time, Pallas kernels for 56%

profile of v1, /device:TPU:1, one launch (start us, length us, event | category | flops | bytes accessed | tf_op | source)
XLA Modules:
  0.0 86.7 jit_solution(8778676072993341865)
XLA Ops:
  0.0 12.0 %time_attention_0.1 = (bf16[8,2,32,768]{3,2,1,0:T(8,128)(2,1)}, bf16[2,512,768]{2,1,0:T(8,128)(2,1)}, bf16[2,512,768]{2,1,0:T(8,128)(2,1)}, bf16[2,256,768]{2,1,0:T(8,128)(2,1)}) custom-call(bf16[2,512,768]{2,1,0:T(8,128)(2,1)} %refs_1_.3, bf16[3,768]{1,0:T(4,128)(2,1)} %gains_hbm.1, f32[512,128]{1,0:T(8,128)} %constant.4.clone.refs_2_, ...), custom_call_target="tpu_custom_call" | custom-call | flops 5234491392 | bytes 8388608 | tf_op jit(solution)/shard_map/time_attention_0/pallas_call | solution.py:304
  12.1 6.8 %all-to-all-start.2 = ((bf16[8,2,32,768]{3,2,1,0:T(8,128)(2,1)}), bf16[8,2,32,768]{3,2,1,0:T(8,128)(2,1)S(1)}, u32[]{:S(2)}, u32[]{:S(2)}) async-start(bf16[8,2,32,768]{3,2,1,0:T(8,128)(2,1)} %get-tuple-element.16), calls=%async_computation.2 | async-start | bytes 1572864 | tf_op jit(solution)/shard_map/all_to_all | solution.py:536
  18.9 11.6 %time_attention_1.1 = (bf16[8,2,32,768]{3,2,1,0:T(8,128)(2,1)}, f32[256,256]{1,0:T(8,128)}) custom-call(s32[256]{0:T(256)} %refs_0_.3, bf16[2,512,768]{2,1,0:T(8,128)(2,1)} %refs_1_.3, f32[512,128]{1,0:T(8,128)} %constant.4.clone.refs_2_, f32[512,128]{1,0:T(8,128)} %constant.5.clone.refs_3_, bf16[768,2304]{1,0:T(8,128)(2,1)} %refs_4_.5, ...), custom_call_target="tpu_custom_call" | custom-call | flops 2818572288 | bytes 8388608 | tf_op jit(solution)/shard_map/time_attention_1/pallas_call | solution.py:304
  30.5 0.7 all-to-all-done.2
  31.2 0.0 copy-start
  31.2 4.3 %all-to-all-start = ((bf16[8,2,32,768]{3,2,1,0:T(8,128)(2,1)}), bf16[8,2,32,768]{3,2,1,0:T(8,128)(2,1)S(1)}, u32[]{:S(2)}, u32[]{:S(2)}) async-start(bf16[8,2,32,768]{3,2,1,0:T(8,128)(2,1)} %get-tuple-element.15), calls=%async_computation | async-start | bytes 1572864 | tf_op jit(solution)/shard_map/all_to_all | solution.py:536
  35.5 0.0 copy-done
  35.5 8.9 %group_attention_0.1 = bf16[16,32,768]{2,1,0:T(8,128)(2,1)} custom-call(f32[256,256]{1,0:T(8,128)} %get-tuple-element.14.refs_0_, bf16[16,32,768]{2,1,0:T(8,128)(2,1)} %bitcast.4, bf16[3,768]{1,0:T(4,128)(2,1)} %gains_hbm.1, bf16[768,2304]{1,0:T(8,128)(2,1)} %refs_3_.5, bf16[768,768]{1,0:T(8,128)(2,1)} %refs_4_.7), custom_call_target="tpu_custom_call" | custom-call | flops 3221225472 | bytes 8388608 | tf_op jit(solution)/shard_map/group_attention_0/pallas_call | solution.py:423
  44.4 3.4 %all-to-all-done = bf16[8,2,32,768]{3,2,1,0:T(8,128)(2,1)S(1)} async-done(((bf16[8,2,32,768]{3,2,1,0:T(8,128)(2,1)}), bf16[8,2,32,768]{3,2,1,0:T(8,128)(2,1)S(1)}, u32[]{:S(2)}, u32[]{:S(2)}) %all-to-all-start) | async-done | bytes 786464 | tf_op jit(solution)/shard_map/all_to_all | solution.py:536
  47.8 0.0 copy-start.1
  47.8 4.3 %all-to-all-start.3 = ((bf16[8,2,32,768]{3,2,1,0:T(8,128)(2,1)}), bf16[8,2,32,768]{3,2,1,0:T(8,128)(2,1)S(1)}, u32[]{:S(2)}, u32[]{:S(2)}) async-start(bf16[8,2,32,768]{3,2,1,0:T(8,128)(2,1)} %bitcast.6), calls=%async_computation.3 | async-start | bytes 1572864 | tf_op jit(solution)/shard_map/all_to_all | solution.py:536
  52.1 0.0 copy-done.1
  52.1 16.3 %group_attention_1.1 = bf16[16,32,768]{2,1,0:T(8,128)(2,1)} custom-call(f32[256,256]{1,0:T(8,128)} %get-tuple-element.14.refs_0_, bf16[16,32,768]{2,1,0:T(8,128)(2,1)} %bitcast.5, bf16[3,768]{1,0:T(4,128)(2,1)} %gains_hbm.1, bf16[768,2304]{1,0:T(8,128)(2,1)} %refs_3_.5, bf16[768,768]{1,0:T(8,128)(2,1)} %refs_4_.7, bf16[768,3072]{1,0:T(8,128)(2,1)} %up_hbm.1, ...), custom_call_target="tpu_custom_call" | custom-call | flops 8053063680 | bytes 8388608 | tf_op jit(solution)/shard_map/group_attention_1/pallas_call | solution.py:423
  68.4 0.0 all-to-all-done.3.x_ref
  68.4 0.0 copy-start.2
  68.4 4.8 %all-to-all-start.1 = ((bf16[8,2,32,768]{3,2,1,0:T(8,128)(2,1)}), bf16[8,2,32,768]{3,2,1,0:T(8,128)(2,1)S(1)}, u32[]{:S(2)}, u32[]{:S(2)}) async-start(bf16[8,2,32,768]{3,2,1,0:T(8,128)(2,1)} %bitcast.7), calls=%async_computation.1 | async-start | bytes 1572864 | tf_op jit(solution)/shard_map/all_to_all | solution.py:536
  73.3 0.0 copy-done.2
  73.3 12.2 %feed_forward_0.1._ = bf16[2,512,768]{2,1,0:T(8,128)(2,1)} custom-call(bf16[8,2,32,768]{3,2,1,0:T(8,128)(2,1)} %copy-done.2, bf16[3,768]{1,0:T(4,128)(2,1)} %gains_hbm.1, bf16[768,3072]{1,0:T(8,128)(2,1)} %up_hbm.1, bf16[3072,768]{1,0:T(8,128)(2,1)} %down_hbm.1), custom_call_target="tpu_custom_call" | custom-call | flops 4831838208 | bytes 4194304 | tf_op jit(solution)/shard_map/feed_forward_0/pallas_call | solution.py:480
  85.4 0.1 all-to-all-done.1.x_ref
  85.6 1.0 %rows_in_place.1 = bf16[2,512,768]{2,1,0:T(8,128)(2,1)} custom-call(bf16[8,2,32,768]{3,2,1,0:T(8,128)(2,1)S(1)} %all-to-all-done.1.x_ref, bf16[2,512,768]{2,1,0:T(8,128)(2,1)} %feed_forward_0.1._), custom_call_target="tpu_custom_call", output_to_operand_aliasing={{}: (1, {})} | custom-call | tf_op jit(solution)/shard_map/rows_in_place/pallas_call | solution.py:519
Async XLA Ops:
  12.1 19.1 %all-to-all-start.2 = ((bf16[8,2,32,768]{3,2,1,0:T(8,128)(2,1)}), bf16[8,2,32,768]{3,2,1,0:T(8,128)(2,1)S(1)}, u32[]{:S(2)}, u32[]{:S(2)}) async-start(bf16[8,2,32,768]{3,2,1,0:T(8,128)(2,1)} %get-tuple-element.16), calls=%async_computation.2 | async-start | bytes 1572864 | tf_op jit(solution)/shard_map/all_to_all | solution.py:536
  31.2 4.3 %copy-start = (bf16[8,2,32,768]{3,2,1,0:T(8,128)(2,1)}, bf16[8,2,32,768]{3,2,1,0:T(8,128)(2,1)S(1)}, u32[]{:S(2)}) copy-start(bf16[8,2,32,768]{3,2,1,0:T(8,128)(2,1)S(1)} %all-to-all-done.2) | copy-start | bytes 2359300
  31.2 16.6 %all-to-all-start = ((bf16[8,2,32,768]{3,2,1,0:T(8,128)(2,1)}), bf16[8,2,32,768]{3,2,1,0:T(8,128)(2,1)S(1)}, u32[]{:S(2)}, u32[]{:S(2)}) async-start(bf16[8,2,32,768]{3,2,1,0:T(8,128)(2,1)} %get-tuple-element.15), calls=%async_computation | async-start | bytes 1572864 | tf_op jit(solution)/shard_map/all_to_all | solution.py:536
  47.8 4.3 %copy-start.1 = (bf16[8,2,32,768]{3,2,1,0:T(8,128)(2,1)}, bf16[8,2,32,768]{3,2,1,0:T(8,128)(2,1)S(1)}, u32[]{:S(2)}) copy-start(bf16[8,2,32,768]{3,2,1,0:T(8,128)(2,1)S(1)} %all-to-all-done) | copy-start | bytes 2359300
  47.8 20.6 %all-to-all-start.3 = ((bf16[8,2,32,768]{3,2,1,0:T(8,128)(2,1)}), bf16[8,2,32,768]{3,2,1,0:T(8,128)(2,1)S(1)}, u32[]{:S(2)}, u32[]{:S(2)}) async-start(bf16[8,2,32,768]{3,2,1,0:T(8,128)(2,1)} %bitcast.6), calls=%async_computation.3 | async-start | bytes 1572864 | tf_op jit(solution)/shard_map/all_to_all | solution.py:536
  68.4 4.8 %copy-start.2 = (bf16[8,2,32,768]{3,2,1,0:T(8,128)(2,1)}, bf16[8,2,32,768]{3,2,1,0:T(8,128)(2,1)S(1)}, u32[]{:S(2)}) copy-start(bf16[8,2,32,768]{3,2,1,0:T(8,128)(2,1)S(1)} %all-to-all-done.3.x_ref) | copy-start | bytes 2359300
  68.4 17.1 %all-to-all-start.1 = ((bf16[8,2,32,768]{3,2,1,0:T(8,128)(2,1)}), bf16[8,2,32,768]{3,2,1,0:T(8,128)(2,1)S(1)}, u32[]{:S(2)}, u32[]{:S(2)}) async-start(bf16[8,2,32,768]{3,2,1,0:T(8,128)(2,1)} %bitcast.7), calls=%async_computation.1 | async-start | bytes 1572864 | tf_op jit(solution)/shard_map/all_to_all | solution.py:536
